TPU v7x, 32 devices: a whole 2x2x4 slice. The times are simulated.
32 devices in a mesh: section: 4 (over y, x), seq: 8 (over z, core).
Axes of the slice: x: 2, y: 2, z: 4, core: 2. Of those that a mesh axis runs over, the one named last changes fastest.
Arguments:
- section_inputs: bfloat16 [4, 2, 4096, 256], P('section', None, 'seq'), may hold values from -6 to 6
- cotangent: bfloat16 [2, 4096, 256], P(None, 'seq'), may hold values from -6 to 6
- conv_weight: bfloat16 [4, 2, 3, 256, 512], P('section'), may hold values from -0.21875 to 0.21875
- out_weight: bfloat16 [4, 2, 256, 256], P('section'), may hold values from -0.375 to 0.375
Outputs:
- input_grads: float32 [4, 2, 4096, 256], P('section', None, 'seq')
- conv_grads: float32 [4, 2, 768, 512], P('section', None, 'seq')
- out_grads: float32 [4, 2, 256, 256], P('section', None, 'seq')
All inputs are finite; a program needn't handle non-finite values.
Results may differ from a plain program's by a relative error of at most 0.019.
Values may be sent and summed in bfloat16 or wider, within the bound.
A program may use at most 128 MiB of HBM per device.

v0:
```python
import functools
import math

import jax
import jax.numpy as jnp
from jax import lax
from jax.experimental import pallas as pl
from jax.experimental.pallas import tpu as pltpu
from jax.sharding import PartitionSpec as P

NEAR = 128
FAR = 1024
CHUNK = 256
MESH = pl.DeviceIdType.MESH
F32 = jnp.float32
BF16 = jnp.bfloat16


def dot_nn(a, b):
    return lax.dot_general(a, b, (((1,), (0,)), ((), ())), preferred_element_type=F32)


def dot_nt(a, b):
    return lax.dot_general(a, b, (((1,), (1,)), ((), ())), preferred_element_type=F32)


def dot_tn(a, b):
    return lax.dot_general(a, b, (((0,), (0,)), ((), ())), preferred_element_type=F32)


def kernel(n, sections, scale, x_ref, cot_ref, cw_ref, ow_ref, ig_ref, cg_ref, og_ref,
           xe, he, fac, gated, gp, gh0, gin, acc, f1s, t1s, f1r, t1r, f0e, t0e, sbuf,
           ct, ot, csend, osend, cpeer, opeer, cpair, opair, crecv, orecv, ssem, rsem):
    micro, rows, chans = x_ref.shape
    depth = cw_ref.shape[0]
    hops = FAR // rows
    near = NEAR
    chips = n // 2
    r = lax.axis_index("seq")
    s = lax.axis_index("section")
    core = lax.rem(r, 2)
    chip = lax.div(r, 2)
    crow, orow = cg_ref.shape[1], og_ref.shape[1]

    counter = [0]
    pending = []

    def make(src, dst, dev, can_send, can_recv):
        i = counter[0]
        counter[0] += 1
        desc = pltpu.make_async_remote_copy(
            src_ref=src, dst_ref=dst, send_sem=ssem.at[i], recv_sem=rsem.at[i],
            device_id=dev, device_id_type=MESH)
        return desc, can_send, can_recv

    def start(item):
        desc, can_send, _ = item
        pending.append(item)
        if can_send is True:
            desc.start()
        else:
            @pl.when(can_send)
            def _():
                desc.start()

    def arrive(item):
        desc, _, can_recv = item
        if can_recv is True:
            desc.wait_recv()
        else:
            @pl.when(can_recv)
            def _():
                desc.wait_recv()

    def at_seq(step):
        return {"seq": lax.rem(r + n + step, n)}

    near_up, near_dn = r < n - 1, r > 0
    far_up, far_dn = r < n - hops, r >= hops
    below = {"section": lax.rem(s + sections - 1, sections)}

    for m in range(micro):
        xe[m, near:near + rows] = x_ref[m]

    @pl.when(s == sections - 1)
    def _():
        gin[...] = cot_ref[...]

    zero = jnp.zeros((near, chans), BF16)
    zrows = jnp.zeros((rows, chans), BF16)

    @pl.when(r == 0)
    def _():
        for m in range(micro):
            xe[m, 0:near] = zero
            t0e[m, 0:near] = zero

    @pl.when(r == n - 1)
    def _():
        for m in range(micro):
            xe[m, near + rows:2 * near + rows] = zero
            f0e[m, rows:rows + near] = zero

    @pl.when(r < hops)
    def _():
        for m in range(micro):
            he[m, 0] = zrows
            t1r[m] = zrows

    @pl.when(r >= n - hops)
    def _():
        for m in range(micro):
            he[m, 2] = zrows
            f1r[m] = zrows

    barrier = pltpu.get_barrier_semaphore()

    def greet(step, carry):
        pl.semaphore_signal(barrier, inc=1, device_id={"seq": lax.rem(r + step, n)},
                            device_id_type=MESH)
        return carry

    lax.fori_loop(1, n, greet, 0)

    @pl.when(s > 0)
    def _():
        pl.semaphore_signal(barrier, inc=1, device_id={"section": s - 1}, device_id_type=MESH)

    @pl.when(s < sections - 1)
    def _():
        pl.semaphore_signal(barrier, inc=1, device_id={"section": s + 1}, device_id_type=MESH)

    at_end = (s == 0) | (s == sections - 1)

    @pl.when(at_end)
    def _():
        pl.semaphore_wait(barrier, n)

    @pl.when(jnp.logical_not(at_end))
    def _():
        pl.semaphore_wait(barrier, n + 1)

    halo = []
    for m in range(micro):
        up = make(xe.at[m, rows:rows + near], xe.at[m, 0:near], at_seq(1), near_up, near_dn)
        dn = make(xe.at[m, near:2 * near], xe.at[m, near + rows:2 * near + rows],
                  at_seq(-1), near_dn, near_up)
        start(up)
        start(dn)
        halo.append((up, dn))

    count = rows // CHUNK
    order = [0, count - 1] + list(range(1, count - 1)) if count > 1 else [0]
    far_h = {}

    def gate(l, m, a, parts):
        pre = dot_nn(parts[0], cw_ref[l, 0])
        pre = pre + dot_nn(parts[1], cw_ref[l, 1])
        pre = pre + dot_nn(parts[2], cw_ref[l, 2])
        t = jnp.tanh(pre[:, :chans])
        sg = 0.5 * jnp.tanh(0.5 * pre[:, chans:]) + 0.5
        ts = t * sg
        fac[l, m, 0, a:a + CHUNK] = (1.0 - t * t) * sg
        fac[l, m, 1, a:a + CHUNK] = ts * (1.0 - sg)
        out = ts.astype(BF16)
        gated[l, m, a:a + CHUNK] = out
        return out

    def forward_near(m):
        for item in halo[m]:
            arrive(item)
        for c in order:
            a = c * CHUNK
            parts = [xe[m, a + k * near:a + k * near + CHUNK] for k in range(3)]
            out = gate(0, m, a, parts)
            nxt = (parts[1].astype(F32) + dot_nn(out, ow_ref[0])).astype(BF16)
            he[m, 1, a:a + CHUNK] = nxt
            up = make(he.at[m, 1, a:a + CHUNK], he.at[m, 0, a:a + CHUNK],
                      at_seq(hops), far_up, far_dn)
            dn = make(he.at[m, 1, a:a + CHUNK], he.at[m, 2, a:a + CHUNK],
                      at_seq(-hops), far_dn, far_up)
            start(up)
            start(dn)
            far_h[m, c] = (up, dn)

    def forward_far(m):
        for c in order:
            a = c * CHUNK
            for item in far_h[m, c]:
                arrive(item)
            gate(1, m, a, [he[m, k, a:a + CHUNK] for k in range(3)])

    relay, far_g, near_g = {}, {}, {}
    for m in range(micro):
        for c in order:
            a = c * CHUNK
            relay[m, c] = make(sbuf.at[m, a:a + CHUNK], gin.at[m, a:a + CHUNK], below,
                               s > 0, s < sections - 1)

    def pre_grad(l, m, a, half):
        gg = dot_nt(half, ow_ref[l])
        gp[l, m, a:a + CHUNK, :chans] = (gg * fac[l, m, 0, a:a + CHUNK]).astype(BF16)
        gp[l, m, a:a + CHUNK, chans:] = (gg * fac[l, m, 1, a:a + CHUNK]).astype(BF16)
        return gp[l, m, a:a + CHUNK]

    def back_far(m, c):
        a = c * CHUNK
        arrive(relay[m, c])
        half = gin[m, a:a + CHUNK]
        grad = pre_grad(1, m, a, half)
        f1s[m, a:a + CHUNK] = dot_nt(grad, cw_ref[1, 0]).astype(BF16)
        dn = make(f1s.at[m, a:a + CHUNK], f1r.at[m, a:a + CHUNK], at_seq(-hops), far_dn, far_up)
        start(dn)
        t1s[m, a:a + CHUNK] = dot_nt(grad, cw_ref[1, 2]).astype(BF16)
        up = make(t1s.at[m, a:a + CHUNK], t1r.at[m, a:a + CHUNK], at_seq(hops), far_up, far_dn)
        start(up)
        far_g[m, c] = (dn, up)
        acc[m, a:a + CHUNK] = half.astype(F32) + dot_nt(grad, cw_ref[1, 1])

    def back_near(m, c):
        a = c * CHUNK
        for item in far_g[m, c]:
            arrive(item)
        flow = acc[m, a:a + CHUNK] + (f1r[m, a:a + CHUNK].astype(F32)
                                      + t1r[m, a:a + CHUNK].astype(F32))
        half = flow.astype(BF16)
        gh0[m, a:a + CHUNK] = half
        grad = pre_grad(0, m, a, half)
        f0e[m, a:a + CHUNK] = dot_nt(grad, cw_ref[0, 0]).astype(BF16)
        if c == 0:
            near_g[m, "hi"] = make(f0e.at[m, 0:near], f0e.at[m, rows:rows + near], at_seq(-1),
                                   near_dn, near_up)
            start(near_g[m, "hi"])
        t0e[m, near + a:near + a + CHUNK] = dot_nt(grad, cw_ref[0, 2]).astype(BF16)
        if c == count - 1:
            near_g[m, "lo"] = make(t0e.at[m, rows:rows + near], t0e.at[m, 0:near], at_seq(1),
                                   near_up, near_dn)
            start(near_g[m, "lo"])
        acc[m, a:a + CHUNK] = flow + dot_nt(grad, cw_ref[0, 1])

    def finish(m, c):
        a = c * CHUNK
        if c == 0:
            arrive(near_g[m, "lo"])
        if c == count - 1:
            arrive(near_g[m, "hi"])
        flow = acc[m, a:a + CHUNK] + (f0e[m, a + near:a + near + CHUNK].astype(F32)
                                      + t0e[m, a:a + CHUNK].astype(F32))
        sbuf[m, a:a + CHUNK] = flow.astype(BF16)
        start(relay[m, c])
        ig_ref[m, a:a + CHUNK] = flow

    def back_near_all(m, between=None):
        done, sent = set(), set()
        for c in order:
            if between is not None:
                between(c)
            back_near(m, c)
            done.add(c)
            for e in order:
                needs = {k for k in (e - 1, e, e + 1) if 0 <= k < count}
                if e not in sent and needs <= done:
                    finish(m, e)
                    sent.add(e)

    def weight_grads(l):
        def tap(k, carry):
            total = None
            for m in range(micro):
                if l == 0:
                    src = xe[m, pl.ds(pl.multiple_of(k * near, near), rows)]
                else:
                    src = he[m, k]
                term = dot_tn(src, gp[l, m])
                total = term if total is None else total + term
            ct[l, pl.ds(pl.multiple_of(k * chans, chans), chans)] = total
            return carry

        lax.fori_loop(0, 3, tap, 0)
        total = None
        for m in range(micro):
            half = gin[m] if l == depth - 1 else gh0[m]
            term = dot_tn(gated[l, m], half)
            total = term if total is None else total + term
        ot[l] = total

    def shard(ref, l, j, size):
        return ref[l, pl.ds(pl.multiple_of(j * size, 8), size)]

    def pair_start(l):
        for i in range(chips):
            j = 2 * i + (1 - core)
            csend[l, i] = shard(ct, l, j, crow).astype(BF16)
            osend[l, i] = shard(ot, l, j, orow).astype(BF16)
        peer = {"seq": r + 1 - 2 * core}
        items = (make(csend.at[l], cpeer.at[l], peer, True, True),
                 make(osend.at[l], opeer.at[l], peer, True, True))
        for item in items:
            start(item)
        return items

    def spread_start(l, items):
        for item in items:
            arrive(item)
        for i in range(chips):
            j = 2 * i + core
            cpair[l, i] = (shard(ct, l, j, crow) + cpeer[l, i].astype(F32)).astype(BF16)
            opair[l, i] = (shard(ot, l, j, orow) + opeer[l, i].astype(F32)).astype(BF16)
        out = []
        for o in range(1, chips):
            other = lax.rem(chip + o, chips)
            dev = {"seq": 2 * other + core}
            pair = (make(cpair.at[l, other], crecv.at[l, o - 1], dev, True, True),
                    make(opair.at[l, other], orecv.at[l, o - 1], dev, True, True))
            for item in pair:
                start(item)
            out.append(pair)
        return out

    def total_up(l, items):
        csum = shard(ct, l, r, crow) + cpeer[l, chip].astype(F32)
        osum = shard(ot, l, r, orow) + opeer[l, chip].astype(F32)
        for o, pair in enumerate(items):
            for item in pair:
                arrive(item)
            csum = csum + crecv[l, o].astype(F32)
            osum = osum + orecv[l, o].astype(F32)
        cg_ref[l] = csum * scale
        og_ref[l] = osum * scale

    for m in range(micro):
        forward_near(m)
    forward_far(0)
    for c in order:
        back_far(0, c)
    for m in range(micro):
        if m + 1 < micro:
            forward_far(m + 1)
            back_near_all(m, functools.partial(back_far, m + 1))
        else:
            back_near_all(m)
    last = depth - 1
    weight_grads(last)
    first_pair = pair_start(last)
    weight_grads(0)
    spread_last = spread_start(last, first_pair)
    second_pair = pair_start(0)
    spread_first = spread_start(0, second_pair)
    total_up(last, spread_last)
    total_up(0, spread_first)
    for desc, can_send, _ in pending:
        if can_send is True:
            desc.wait_send()
        else:
            @pl.when(can_send)
            def _(desc=desc):
                desc.wait_send()


def shards(section_inputs, cotangent, conv_weight, out_weight):
    n = lax.axis_size("seq")
    sections = lax.axis_size("section")
    micro, rows, chans = cotangent.shape
    depth = conv_weight.shape[1]
    scale = 1.0 / math.sqrt(micro * rows * n)
    chips = n // 2
    crow, orow = 3 * chans // n, chans // n
    count = rows // CHUNK
    sems = micro * (2 + 2 * count + 2 * count + 2 + count) + depth * (2 + 2 * (chips - 1))
    plane = lambda *d: pltpu.VMEM((*d, rows, chans), BF16)
    scratch = [
        pltpu.VMEM((micro, rows + 2 * NEAR, chans), BF16),
        plane(micro, 3),
        pltpu.VMEM((depth, micro, 2, rows, chans), F32),
        plane(depth, micro),
        pltpu.VMEM((depth, micro, rows, 2 * chans), BF16),
        plane(micro),
        plane(micro),
        pltpu.VMEM((micro, rows, chans), F32),
        plane(micro), plane(micro), plane(micro), plane(micro),
        pltpu.VMEM((micro, rows + NEAR, chans), BF16),
        pltpu.VMEM((micro, rows + NEAR, chans), BF16),
        plane(micro),
        pltpu.VMEM((depth, 3 * chans, 2 * chans), F32),
        pltpu.VMEM((depth, chans, chans), F32),
    ]
    for lead in (chips, chips, chips, chips - 1):
        scratch.append(pltpu.VMEM((depth, lead, crow, 2 * chans), BF16))
        scratch.append(pltpu.VMEM((depth, lead, orow, chans), BF16))
    scratch += [pltpu.SemaphoreType.DMA((sems,)), pltpu.SemaphoreType.DMA((sems,))]
    ig, cg, og = pl.pallas_call(
        functools.partial(kernel, n, sections, scale),
        out_shape=(
            jax.ShapeDtypeStruct((micro, rows, chans), F32),
            jax.ShapeDtypeStruct((depth, crow, 2 * chans), F32),
            jax.ShapeDtypeStruct((depth, orow, chans), F32),
        ),
        in_specs=[pl.BlockSpec(memory_space=pltpu.VMEM)] * 4,
        out_specs=(pl.BlockSpec(memory_space=pltpu.VMEM),) * 3,
        scratch_shapes=scratch,
        compiler_params=pltpu.CompilerParams(
            collective_id=0, has_side_effects=True, vmem_limit_bytes=56 * 2**20
        ),
    )(section_inputs[0], cotangent, conv_weight[0], out_weight[0])
    return ig[None], cg[None], og[None]


def solution(mesh):
    return jax.shard_map(
        shards,
        mesh=mesh,
        in_specs=(
            P("section", None, "seq", None),
            P(None, "seq", None),
            P("section", None, None, None, None),
            P("section", None, None, None),
        ),
        out_specs=(
            P("section", None, "seq", None),
            P("section", None, "seq", None),
            P("section", None, "seq", None),
        ),
        check_vma=False,
    )
```

profile of v0, /device:TPU:9, one launch (start us, length us, event | category | flops | bytes accessed | tf_op | source)
XLA Modules:
  0.0 119.7 jit_solution(2195114293231273817)
XLA Ops:
  0.6 115.4 %shard_map.67 = (f32[2,512,256]{2,1,0:T(8,128)}, f32[2,96,512]{2,1,0:T(8,128)}, f32[2,32,256]{2,1,0:T(8,128)}) custom-call(bf16[2,512,256]{2,1,0:T(8,128)(2,1)} %bitcast.8, bf16[2,512,256]{2,1,0:T(8,128)(2,1)} %cot_ref.1, bf16[2,3,256,512]{3,2,1,0:T(8,128)(2,1)} %bitcast.6, bf16[2,256,256]{2,1,0:T(8,128)(2,1)} %bitcast.10), custom_call_target="tpu_custom_call" | custom-call | tf_op jit(solution)/shard_map/pallas_call | solution.py:391
  116.0 0.0 copy-start
  116.0 0.0 copy-start.1
  116.0 2.3 %copy.10 = f32[1,2,512,256]{3,2,1,0:T(8,128)} copy(f32[1,2,512,256]{3,2,1,0:T(8,128)} %bitcast.7) | data formatting | bytes 2097152
  118.3 0.0 copy-done
  118.3 0.7 copy.11
  119.1 0.0 copy-done.1
  119.1 0.6 copy.12
Async XLA Ops:
  116.0 2.3 %copy-start = (f32[2,96,512]{2,1,0:T(8,128)S(1)}, f32[2,96,512]{2,1,0:T(8,128)}, u32[]{:S(2)}) copy-start(f32[2,96,512]{2,1,0:T(8,128)} %get-tuple-element.7) | copy-start | bytes 1179652
  116.0 3.1 %copy-start.1 = (f32[2,32,256]{2,1,0:T(8,128)S(1)}, f32[2,32,256]{2,1,0:T(8,128)}, u32[]{:S(2)}) copy-start(f32[2,32,256]{2,1,0:T(8,128)} %get-tuple-element.8) | copy-start | bytes 196612
where the time goes:
time: 120 us
  Pallas kernels  115 us (96%)
  local copies, waits for them, and re-layouts  3.7 us (3%)
    pallas_call x1, Pallas kernels, shards(): pl.pallas_call(functools.partial(kernel, n, sections, scale), out_shape=(...  115 us
    unnamed x7, local copies, waits for them, and re-layouts  3.7 us

commit v1 on v0

--- a/solution.py
+++ b/solution.py
@@ -10,7 +10,7 @@
 
 NEAR = 128
 FAR = 1024
-CHUNK = 256
+CHUNK = 128
 MESH = pl.DeviceIdType.MESH
 F32 = jnp.float32
 BF16 = jnp.bfloat16
@@ -20,17 +20,13 @@
     return lax.dot_general(a, b, (((1,), (0,)), ((), ())), preferred_element_type=F32)
 
 
-def dot_nt(a, b):
-    return lax.dot_general(a, b, (((1,), (1,)), ((), ())), preferred_element_type=F32)
-
-
 def dot_tn(a, b):
     return lax.dot_general(a, b, (((0,), (0,)), ((), ())), preferred_element_type=F32)
 
 
 def kernel(n, sections, scale, x_ref, cot_ref, cw_ref, ow_ref, ig_ref, cg_ref, og_ref,
            xe, he, fac, gated, gp, gh0, gin, acc, f1s, t1s, f1r, t1r, f0e, t0e, sbuf,
-           ct, ot, csend, osend, cpeer, opeer, cpair, opair, crecv, orecv, ssem, rsem):
+           ct, ot, csend, osend, cpeer, opeer, cpair, opair, crecv, orecv, cwt, owt, ssem, rsem):
     micro, rows, chans = x_ref.shape
     depth = cw_ref.shape[0]
     hops = FAR // rows
@@ -51,11 +47,11 @@
         desc = pltpu.make_async_remote_copy(
             src_ref=src, dst_ref=dst, send_sem=ssem.at[i], recv_sem=rsem.at[i],
             device_id=dev, device_id_type=MESH)
-        return desc, can_send, can_recv
+        pending.append((desc, can_send, can_recv))
+        return pending[-1]
 
     def start(item):
         desc, can_send, _ = item
-        pending.append(item)
         if can_send is True:
             desc.start()
         else:
@@ -148,6 +144,11 @@
         start(up)
         start(dn)
         halo.append((up, dn))
+
+    for l in range(depth):
+        owt[l] = ow_ref[l].T
+        for k in range(3):
+            cwt[l, k] = cw_ref[l, k].T
 
     count = rows // CHUNK
     order = [0, count - 1] + list(range(1, count - 1)) if count > 1 else [0]
@@ -175,13 +176,8 @@
             out = gate(0, m, a, parts)
             nxt = (parts[1].astype(F32) + dot_nn(out, ow_ref[0])).astype(BF16)
             he[m, 1, a:a + CHUNK] = nxt
-            up = make(he.at[m, 1, a:a + CHUNK], he.at[m, 0, a:a + CHUNK],
-                      at_seq(hops), far_up, far_dn)
-            dn = make(he.at[m, 1, a:a + CHUNK], he.at[m, 2, a:a + CHUNK],
-                      at_seq(-hops), far_dn, far_up)
-            start(up)
-            start(dn)
-            far_h[m, c] = (up, dn)
+            for item in far_h[m, c]:
+                start(item)
 
     def forward_far(m):
         for c in order:
@@ -192,13 +188,30 @@
 
     relay, far_g, near_g = {}, {}, {}
     for m in range(micro):
+        near_g[m, "hi"] = make(f0e.at[m, 0:near], f0e.at[m, rows:rows + near], at_seq(-1),
+                               near_dn, near_up)
+        near_g[m, "lo"] = make(t0e.at[m, rows:rows + near], t0e.at[m, 0:near], at_seq(1),
+                               near_up, near_dn)
+        for c in order:
+            a = c * CHUNK
+            far_h[m, c] = (
+                make(he.at[m, 1, a:a + CHUNK], he.at[m, 0, a:a + CHUNK],
+                     at_seq(hops), far_up, far_dn),
+                make(he.at[m, 1, a:a + CHUNK], he.at[m, 2, a:a + CHUNK],
+                     at_seq(-hops), far_dn, far_up))
+            far_g[m, c] = (
+                make(f1s.at[m, a:a + CHUNK], f1r.at[m, a:a + CHUNK],
+                     at_seq(-hops), far_dn, far_up),
+                make(t1s.at[m, a:a + CHUNK], t1r.at[m, a:a + CHUNK],
+                     at_seq(hops), far_up, far_dn))
+    for m in range(micro):
         for c in order:
             a = c * CHUNK
             relay[m, c] = make(sbuf.at[m, a:a + CHUNK], gin.at[m, a:a + CHUNK], below,
                                s > 0, s < sections - 1)
 
     def pre_grad(l, m, a, half):
-        gg = dot_nt(half, ow_ref[l])
+        gg = dot_nn(half, owt[l])
         gp[l, m, a:a + CHUNK, :chans] = (gg * fac[l, m, 0, a:a + CHUNK]).astype(BF16)
         gp[l, m, a:a + CHUNK, chans:] = (gg * fac[l, m, 1, a:a + CHUNK]).astype(BF16)
         return gp[l, m, a:a + CHUNK]
@@ -208,14 +221,11 @@
         arrive(relay[m, c])
         half = gin[m, a:a + CHUNK]
         grad = pre_grad(1, m, a, half)
-        f1s[m, a:a + CHUNK] = dot_nt(grad, cw_ref[1, 0]).astype(BF16)
-        dn = make(f1s.at[m, a:a + CHUNK], f1r.at[m, a:a + CHUNK], at_seq(-hops), far_dn, far_up)
-        start(dn)
-        t1s[m, a:a + CHUNK] = dot_nt(grad, cw_ref[1, 2]).astype(BF16)
-        up = make(t1s.at[m, a:a + CHUNK], t1r.at[m, a:a + CHUNK], at_seq(hops), far_up, far_dn)
-        start(up)
-        far_g[m, c] = (dn, up)
-        acc[m, a:a + CHUNK] = half.astype(F32) + dot_nt(grad, cw_ref[1, 1])
+        f1s[m, a:a + CHUNK] = dot_nn(grad, cwt[1, 0]).astype(BF16)
+        start(far_g[m, c][0])
+        t1s[m, a:a + CHUNK] = dot_nn(grad, cwt[1, 2]).astype(BF16)
+        start(far_g[m, c][1])
+        acc[m, a:a + CHUNK] = half.astype(F32) + dot_nn(grad, cwt[1, 1])
 
     def back_near(m, c):
         a = c * CHUNK
@@ -226,17 +236,13 @@
         half = flow.astype(BF16)
         gh0[m, a:a + CHUNK] = half
         grad = pre_grad(0, m, a, half)
-        f0e[m, a:a + CHUNK] = dot_nt(grad, cw_ref[0, 0]).astype(BF16)
+        f0e[m, a:a + CHUNK] = dot_nn(grad, cwt[0, 0]).astype(BF16)
         if c == 0:
-            near_g[m, "hi"] = make(f0e.at[m, 0:near], f0e.at[m, rows:rows + near], at_seq(-1),
-                                   near_dn, near_up)
             start(near_g[m, "hi"])
-        t0e[m, near + a:near + a + CHUNK] = dot_nt(grad, cw_ref[0, 2]).astype(BF16)
+        t0e[m, near + a:near + a + CHUNK] = dot_nn(grad, cwt[0, 2]).astype(BF16)
         if c == count - 1:
-            near_g[m, "lo"] = make(t0e.at[m, rows:rows + near], t0e.at[m, 0:near], at_seq(1),
-                                   near_up, near_dn)
             start(near_g[m, "lo"])
-        acc[m, a:a + CHUNK] = flow + dot_nt(grad, cw_ref[0, 1])
+        acc[m, a:a + CHUNK] = flow + dot_nn(grad, cwt[0, 1])
 
     def finish(m, c):
         a = c * CHUNK
@@ -287,35 +293,36 @@
     def shard(ref, l, j, size):
         return ref[l, pl.ds(pl.multiple_of(j * size, 8), size)]
 
+    peer = {"seq": r + 1 - 2 * core}
+    pairs, spread = {}, {}
+    for l in range(depth):
+        pairs[l] = (make(csend.at[l], cpeer.at[l], peer, True, True),
+                    make(osend.at[l], opeer.at[l], peer, True, True))
+        spread[l] = []
+        for o in range(1, chips):
+            other = lax.rem(chip + o, chips)
+            dev = {"seq": 2 * other + core}
+            spread[l].append((make(cpair.at[l, other], crecv.at[l, o - 1], dev, True, True),
+                              make(opair.at[l, other], orecv.at[l, o - 1], dev, True, True)))
+
     def pair_start(l):
         for i in range(chips):
             j = 2 * i + (1 - core)
             csend[l, i] = shard(ct, l, j, crow).astype(BF16)
             osend[l, i] = shard(ot, l, j, orow).astype(BF16)
-        peer = {"seq": r + 1 - 2 * core}
-        items = (make(csend.at[l], cpeer.at[l], peer, True, True),
-                 make(osend.at[l], opeer.at[l], peer, True, True))
-        for item in items:
+        for item in pairs[l]:
             start(item)
-        return items
-
-    def spread_start(l, items):
-        for item in items:
+
+    def spread_start(l):
+        for item in pairs[l]:
             arrive(item)
         for i in range(chips):
             j = 2 * i + core
             cpair[l, i] = (shard(ct, l, j, crow) + cpeer[l, i].astype(F32)).astype(BF16)
             opair[l, i] = (shard(ot, l, j, orow) + opeer[l, i].astype(F32)).astype(BF16)
-        out = []
-        for o in range(1, chips):
-            other = lax.rem(chip + o, chips)
-            dev = {"seq": 2 * other + core}
-            pair = (make(cpair.at[l, other], crecv.at[l, o - 1], dev, True, True),
-                    make(opair.at[l, other], orecv.at[l, o - 1], dev, True, True))
+        for pair in spread[l]:
             for item in pair:
                 start(item)
-            out.append(pair)
-        return out
 
     def total_up(l, items):
         csum = shard(ct, l, r, crow) + cpeer[l, chip].astype(F32)
@@ -328,26 +335,44 @@
         cg_ref[l] = csum * scale
         og_ref[l] = osum * scale
 
-    for m in range(micro):
-        forward_near(m)
-    forward_far(0)
-    for c in order:
-        back_far(0, c)
-    for m in range(micro):
-        if m + 1 < micro:
-            forward_far(m + 1)
+    top = s == sections - 1
+    last, end = depth - 1, micro - 1
+
+    @pl.when(top)
+    def _():
+        for m in range(micro):
+            if m == 0:
+                forward_near(0)
+            forward_far(m)
+            for c in order:
+                back_far(m, c)
+            if m < end:
+                forward_near(m + 1)
+                back_near_all(m)
+
+    @pl.when(jnp.logical_not(top))
+    def _():
+        for m in range(micro):
+            forward_near(m)
+        for m in range(micro):
+            forward_far(m)
+        for c in order:
+            back_far(0, c)
+        for m in range(end):
             back_near_all(m, functools.partial(back_far, m + 1))
-        else:
-            back_near_all(m)
-    last = depth - 1
-    weight_grads(last)
-    first_pair = pair_start(last)
+
+    def reduce_last():
+        weight_grads(last)
+        pair_start(last)
+        spread_start(last)
+
+    back_near_all(end)
+    reduce_last()
     weight_grads(0)
-    spread_last = spread_start(last, first_pair)
-    second_pair = pair_start(0)
-    spread_first = spread_start(0, second_pair)
-    total_up(last, spread_last)
-    total_up(0, spread_first)
+    pair_start(0)
+    spread_start(0)
+    total_up(last, spread[last])
+    total_up(0, spread[0])
     for desc, can_send, _ in pending:
         if can_send is True:
             desc.wait_send()
@@ -387,6 +412,10 @@
     for lead in (chips, chips, chips, chips - 1):
         scratch.append(pltpu.VMEM((depth, lead, crow, 2 * chans), BF16))
         scratch.append(pltpu.VMEM((depth, lead, orow, chans), BF16))
+    scratch += [
+        pltpu.VMEM((depth, 3, 2 * chans, chans), BF16),
+        pltpu.VMEM((depth, chans, chans), BF16),
+    ]
     scratch += [pltpu.SemaphoreType.DMA((sems,)), pltpu.SemaphoreType.DMA((sems,))]
     ig, cg, og = pl.pallas_call(
         functools.partial(kernel, n, sections, scale),

time: 120 us -> 114 us (0.950)
  Pallas kernels: 115 us -> 110 us
    pallas_call x1, Pallas kernels: 115 us -> 110 us  [shards(): pl.pallas_call(functools.partial(kernel, n, sections, scale), out_shape=(...]
where the time goes in v1:
time: 114 us
  Pallas kernels  110 us (96%)
  local copies, waits for them, and re-layouts  3.7 us (3%)
    pallas_call x1, Pallas kernels, shards(): pl.pallas_call(functools.partial(kernel, n, sections, scale), out_shape=(...  110 us
    unnamed x7, local copies, waits for them, and re-layouts  3.7 us

profile of v1, /device:TPU:9, one launch (start us, length us, event | category | flops | bytes accessed | tf_op | source)
XLA Modules:
  0.0 114.1 jit_solution(2195504228992834371)
XLA Ops:
  0.6 109.8 %shard_map.67 = (f32[2,512,256]{2,1,0:T(8,128)}, f32[2,96,512]{2,1,0:T(8,128)}, f32[2,32,256]{2,1,0:T(8,128)}) custom-call(bf16[2,512,256]{2,1,0:T(8,128)(2,1)} %bitcast.8, bf16[2,512,256]{2,1,0:T(8,128)(2,1)} %cot_ref.1, bf16[2,3,256,512]{3,2,1,0:T(8,128)(2,1)} %bitcast.6, bf16[2,256,256]{2,1,0:T(8,128)(2,1)} %bitcast.10), custom_call_target="tpu_custom_call" | custom-call | tf_op jit(solution)/shard_map/pallas_call | solution.py:420
  110.4 0.0 copy-start
  110.4 0.0 copy-start.1
  110.4 2.3 %copy.10 = f32[1,2,512,256]{3,2,1,0:T(8,128)} copy(f32[1,2,512,256]{3,2,1,0:T(8,128)} %bitcast.7) | data formatting | bytes 2097152
  112.7 0.0 copy-done
  112.7 0.7 copy.11
  113.5 0.0 copy-done.1
  113.5 0.6 copy.12
Async XLA Ops:
  110.4 2.3 %copy-start = (f32[2,96,512]{2,1,0:T(8,128)S(1)}, f32[2,96,512]{2,1,0:T(8,128)}, u32[]{:S(2)}) copy-start(f32[2,96,512]{2,1,0:T(8,128)} %get-tuple-element.7) | copy-start | bytes 1179652
  110.4 3.1 %copy-start.1 = (f32[2,32,256]{2,1,0:T(8,128)S(1)}, f32[2,32,256]{2,1,0:T(8,128)}, u32[]{:S(2)}) copy-start(f32[2,32,256]{2,1,0:T(8,128)} %get-tuple-element.8) | copy-start | bytes 196612

commit v2 on v1

--- a/solution.py
+++ b/solution.py
@@ -356,10 +356,11 @@
             forward_near(m)
         for m in range(micro):
             forward_far(m)
-        for c in order:
-            back_far(0, c)
-        for m in range(end):
-            back_near_all(m, functools.partial(back_far, m + 1))
+        for m in range(micro):
+            for c in order:
+                back_far(m, c)
+            if m < end:
+                back_near_all(m)
 
     def reduce_last():
         weight_grads(last)

time: 114 us -> 108 us (0.947)
  Pallas kernels: 110 us -> 103 us
    pallas_call x1, Pallas kernels: 110 us -> 103 us  [shards(): pl.pallas_call(functools.partial(kernel, n, sections, scale), out_shape=(...]
where the time goes in v2:
time: 108 us
  Pallas kernels  103 us (95%)
  local copies, waits for them, and re-layouts  3.7 us (3%)
    pallas_call x1, Pallas kernels, shards(): pl.pallas_call(functools.partial(kernel, n, sections, scale), out_shape=(...  103 us
    unnamed x7, local copies, waits for them, and re-layouts  3.7 us

profile of v2, /device:TPU:9, one launch (start us, length us, event | category | flops | bytes accessed | tf_op | source)
XLA Modules:
  0.0 107.6 jit_solution(6736600736855327143)
XLA Ops:
  0.6 103.2 %shard_map.67 = (f32[2,512,256]{2,1,0:T(8,128)}, f32[2,96,512]{2,1,0:T(8,128)}, f32[2,32,256]{2,1,0:T(8,128)}) custom-call(bf16[2,512,256]{2,1,0:T(8,128)(2,1)} %bitcast.8, bf16[2,512,256]{2,1,0:T(8,128)(2,1)} %cot_ref.1, bf16[2,3,256,512]{3,2,1,0:T(8,128)(2,1)} %bitcast.6, bf16[2,256,256]{2,1,0:T(8,128)(2,1)} %bitcast.10), custom_call_target="tpu_custom_call" | custom-call | tf_op jit(solution)/shard_map/pallas_call | solution.py:421
  103.9 0.0 copy-start
  103.9 0.0 copy-start.1
  103.9 2.3 %copy.10 = f32[1,2,512,256]{3,2,1,0:T(8,128)} copy(f32[1,2,512,256]{3,2,1,0:T(8,128)} %bitcast.7) | data formatting | bytes 2097152
  106.2 0.0 copy-done
  106.2 0.7 copy.11
  107.0 0.0 copy-done.1
  107.0 0.6 copy.12
Async XLA Ops:
  103.9 2.3 %copy-start = (f32[2,96,512]{2,1,0:T(8,128)S(1)}, f32[2,96,512]{2,1,0:T(8,128)}, u32[]{:S(2)}) copy-start(f32[2,96,512]{2,1,0:T(8,128)} %get-tuple-element.7) | copy-start | bytes 1179652
  103.9 3.1 %copy-start.1 = (f32[2,32,256]{2,1,0:T(8,128)S(1)}, f32[2,32,256]{2,1,0:T(8,128)}, u32[]{:S(2)}) copy-start(f32[2,32,256]{2,1,0:T(8,128)} %get-tuple-element.8) | copy-start | bytes 196612
